TPU v7x, 256 devices: a whole 4x4x8 slice. The times are simulated.
256 devices in a mesh: pr: 16 (over x, z_lo, core), pc: 16 (over y, z_hi).
Axes of the slice: x: 4, y: 4, z: 8 (z_hi: 4, z_lo: 2; z = z_hi * 2 + z_lo), core: 2. Of those that a mesh axis runs over, the one named last changes fastest.
Arguments:
- root_inverse: float32 [8192, 8192], P('pr', 'pc'), may hold values from -12 to 12
- panels: float32 [2, 4096, 2048], P(None, 'pr', 'pc'), may hold values from -0.09375 to 0.09375
- child_rows: int32 [2, 16], replicated, may hold values from 0 to 31, as said below
- block_inverse: float32 [2, 2048, 2048], P(None, 'pc', 'pr'), may hold values from -6 to 6
Outputs:
- coupling: float32 [2, 8192, 2048], P(None, 'pc', 'pr')
- diagonal: float32 [2, 2048, 2048], P(None, 'pc', 'pr')
Inputs may be any that keep to these rules, and one draw needn't show every extreme that they name: `child_rows`: each row holds 16 distinct block indices in no particular order, always including 0 and 31.
All inputs are finite; a program needn't handle non-finite values.
Results may differ from a plain program's by a relative error of at most 0.0001.
Values sent between devices are 32-bit elements; how exact they have to be, the bound alone decides.
A program may use at most 128 MiB of HBM per device.

v0:
```python
import jax
import jax.numpy as jnp
from jax import lax
from jax.sharding import PartitionSpec as P

BLOCK = 256


exact = lax.Precision.HIGHEST


def body(root_inverse, panels, child_rows, block_inverse):
    inverse_rows, inverse_cols = root_inverse.shape
    panel_width = panels.shape[2]
    list_length = child_rows.shape[1]
    grid_row = lax.axis_index("pr")
    compact = lax.all_gather(panels, "pr", axis=1, tiled=True)
    blocks_compact = compact.reshape(2, list_length, BLOCK, panel_width)
    local_count = inverse_rows // BLOCK
    local_blocks = grid_row * local_count + jnp.arange(local_count, dtype=jnp.int32)
    selector = (child_rows[:, None, :] == local_blocks[None, :, None]).astype(jnp.float32)
    expanded = jnp.einsum("cbt,ctkw->cbkw", selector, blocks_compact, precision=exact).reshape(
        2, inverse_rows, panel_width
    )
    products_sum = -jnp.einsum(
        "ji,cjn->cin",
        root_inverse,
        lax.all_gather(expanded, "pc", axis=2, tiled=True),
        precision=exact,
    )
    coupling = lax.psum_scatter(products_sum, "pr", scatter_dimension=2, tiled=True)
    within = jnp.arange(BLOCK, dtype=jnp.int32)
    source_rows = (child_rows[:, :, None] * BLOCK + within[None, None, :]).reshape(
        2, list_length * BLOCK
    )
    portion = lax.all_gather(coupling, "pc", axis=1, tiled=True)
    height = portion.shape[1]
    inside = (source_rows >= 0) & (source_rows < height)
    clipped = jnp.clip(source_rows, 0, height - 1)
    taken = jnp.take_along_axis(portion, clipped[:, :, None], axis=1)
    selected = jnp.where(inside[:, :, None], taken, 0.0)
    panel_terms = jnp.einsum("ctx,cty->cxy", compact, selected, precision=exact)
    diagonal = block_inverse - panel_terms
    return (coupling, diagonal)


def solution(mesh):
    in_specs = (P("pr", "pc"), P(None, "pr", "pc"), P(), P(None, "pc", "pr"))
    out_specs = (P(None, "pc", "pr"), P(None, "pc", "pr"))
    return jax.shard_map(body, mesh=mesh, in_specs=in_specs, out_specs=out_specs, check_vma=False)
```

profile of v0, /device:TPU:35, one launch (start us, length us, event | category | flops | bytes accessed | tf_op | source)
XLA Modules:
  0.0 558.5 jit_solution(14459076657078958008)
XLA Ops:
  7.2 0.0 all-gather.4.cloned.1.call-start
  7.2 0.7 all-gather.4.cloned.1.call-update
  7.9 0.0 all-gather.6.cloned.1.call-start
  8.0 43.8 %all-gather.4.cloned.1.call-done = f32[2,4096,128]{2,1,0:T(8,128)} async-done(((f32[2,256,128]{2,1,0:T(8,128)}), f32[2,4096,128]{2,1,0:T(8,128)}) %all-gather.4.cloned.1.call-update) | async-done | bytes 4194320 | tf_op jit(solution)/shard_map/all_gather | solution.py:17
  51.7 5.9 %fusion = f32[2,2,256,128]{3,1,2,0:T(2,128)S(1)} fusion(f32[2,16,256,128]{3,2,1,0:T(8,128)} %bitcast.31, s32[2,16]{1,0:T(2,128)} %param.6, s32[2]{0:T(128)S(1)} %iota_add_fusion), kind=kOutput, calls=%fused_computation.2 | convolution fusion | flops 25165888 | bytes 4718728 | tf_op jit(solution)/shard_map/cbt,ctkw->cbkw/dot_general | solution.py:22
  57.7 1.0 copy.13
  58.7 0.0 all-gather.6.cloned.1.call-update
  58.7 0.0 reduce-scatter.2.cloned.1.call-start
  58.7 117.9 %all-gather.6.cloned.1.call-done = f32[2,512,2048]{1,2,0:T(8,128)} async-done(((f32[2,512,128]{1,2,0:T(8,128)}), f32[2,512,2048]{1,2,0:T(8,128)}) %all-gather.6.cloned.1.call-update) | async-done | bytes 8388624 | tf_op jit(solution)/shard_map/all_gather | solution.py:28
  176.6 17.2 %negate_bitcast_fusion = f32[2,512,2048]{1,2,0:T(8,128)} fusion(f32[2,512,2048]{1,2,0:T(8,128)} %all-gather.6.cloned.1.call-done, f32[512,512]{1,0:T(8,128)S(1)} %copy-done), kind=kOutput, calls=%fused_computation.1 | convolution fusion | flops 12886999040 | bytes 17825792 | tf_op jit(solution)/shard_map/ji,cjn->cin/dot_general | solution.py:25
  193.9 0.2 all-gather.8.cloned.1.call-start
  194.1 95.9 %reduce-scatter.2.cloned.1.call-done = f32[2,512,128]{1,2,0:T(8,128)} async-done(((f32[2,512,2048]{1,2,0:T(8,128)}), f32[2,512,128]{1,2,0:T(8,128)}) %reduce-scatter.2.cloned.1.call-update) | async-done | bytes 524304 | tf_op jit(solution)/shard_map/reduce_scatter | solution.py:31
  290.0 0.1 add.74
  290.1 0.1 fusion.19
  290.2 0.1 broadcast_bitcast_fusion
  290.3 0.1 copy.16
  290.4 0.1 compare_and_fusion.1
  290.5 2.0 copy.17
  292.6 117.5 %all-gather.8.cloned.1.call-done = f32[2,8192,128]{1,2,0:T(8,128)} async-done(((f32[2,512,128]{1,2,0:T(8,128)}), f32[2,8192,128]{1,2,0:T(8,128)}) %all-gather.8.cloned.1.call-update) | async-done | bytes 8388624 | tf_op jit(solution)/shard_map/all_gather | solution.py:36
  410.1 8.8 %copy.14 = f32[2,8192,128]{2,1,0:T(8,128)} copy(f32[2,8192,128]{1,2,0:T(8,128)} %all-gather.8.cloned.1.call-done) | data formatting | bytes 16777216 | tf_op jit(solution)/shard_map/all_gather | solution.py:36
  418.9 118.7 %gather_fusion = f32[8192,128]{1,0:T(8,128)} fusion(f32[2,8192,128]{2,1,0:T(8,128)} %copy.14, s32[8192]{0:T(1024)S(1)} %bitcast.29), kind=kCustom, calls=%fused_computation | custom fusion | bytes 8454144 | tf_op jit(solution)/shard_map/jit(take_along_axis)/gather | solution.py:40
  537.7 5.7 %copy.15 = f32[2,4096,128]{1,2,0:T(8,128)} copy(f32[2,4096,128]{2,1,0:T(8,128)} %bitcast.30) | data formatting | bytes 8388608 | tf_op jit(solution)/shard_map/jit(take_along_axis)/gather | solution.py:40
  543.3 7.9 %fusion.12 = f32[2,128,128]{1,2,0:T(8,128)S(1)} fusion(f32[2,128,128]{1,2,0:T(8,128)S(1)} %copy.16, f32[2,4096,128]{2,1,0:T(8,128)} %all-gather.4.cloned.1.call-done, f32[2,4096,128]{1,2,0:T(8,128)} %copy.15, pred[2,4096]{1,0:T(4,128)(4,1)S(1)} %get-tuple-element.7, pred[2,4096]{1,0:T(4,128)(4,1)S(1)} %get-tuple-element.6), kind=kOutput, calls=%fused_computation.12 | convolution fusion | flops 1612742656 | bytes 8667136 | tf_op jit(solution)/shard_map/ctx,cty->cxy/dot_general | solution.py:42
  551.2 0.8 copy.18
  (16 shorter events, 0.2 us)
Async XLA Ops:
  7.2 169.4 %copy-start = (f32[512,512]{1,0:T(8,128)S(1)}, f32[512,512]{1,0:T(8,128)}, u32[]{:S(2)}) copy-start(f32[512,512]{1,0:T(8,128)} %param.4) | copy-start | bytes 3145732
  7.2 44.6 %all-gather.4.cloned.1.call-start = ((), (), s32[]{:S(2)}) async-start(), calls=%async_computation.1 | async-start | bytes 4456448 | tf_op jit(solution)/shard_map/all_gather | solution.py:17
  7.9 168.7 %all-gather.6.cloned.1.call-start = ((), (), s32[]{:S(2)}) async-start(), calls=%async_computation.2 | async-start | bytes 8912896 | tf_op jit(solution)/shard_map/all_gather | solution.py:28
  58.7 231.3 %reduce-scatter.2.cloned.1.call-start = ((), (), s32[]{:S(2)}) async-start(), calls=%async_computation.3 | async-start | bytes 8912896 | tf_op jit(solution)/shard_map/reduce_scatter | solution.py:31
  193.8 96.2 %copy-start.2 = (s32[2,16]{1,0:T(2,128)S(1)}, s32[2,16]{1,0:T(2,128)}, u32[]{:S(2)}) copy-start(s32[2,16]{1,0:T(2,128)} %param.6) | copy-start | bytes 388
  193.8 96.5 %copy-start.1 = (f32[2,128,128]{2,1,0:T(8,128)S(1)}, f32[2,128,128]{2,1,0:T(8,128)}, u32[]{:S(2)}) copy-start(f32[2,128,128]{2,1,0:T(8,128)} %param.7) | copy-start | bytes 393220
  193.9 216.2 %all-gather.8.cloned.1.call-start = ((), (), s32[]{:S(2)}) async-start(), calls=%async_computation.4 | async-start | bytes 8912896 | tf_op jit(solution)/shard_map/all_gather | solution.py:36
Sparse Core Ops, SparseCore 0:
  9.8 41.8 all-gather.3
  58.8 117.7 all-gather.5
  194.0 95.9 reduce-scatter.1
  292.3 117.7 all-gather.7
where the time goes:
time: 560 us; the launch traced here: 559 us
  waiting for transfers between devices  376 us (67%)
  local copies, waits for them, and re-layouts  137 us (24%)
  matrix products  31 us (6%)
  between operations  13.9 us (2%)
    gather x2, local copies, waits for them, and re-layouts, body(): taken = jnp.take_along_axis(portion, clipped[:, :, None], axis=1)  124 us
    all_gather x1, waiting for transfers between devices, body(): lax.all_gather(expanded, 'pc', axis=2, tiled=True)  118 us
    all_gather x1, waiting for transfers between devices, body(): portion = lax.all_gather(coupling, 'pc', axis=1, tiled=True)  118 us
    reduce_scatter x1, waiting for transfers between devices, body(): lax.psum_scatter(products_sum, 'pr', scatter_dimension=2, tiled=True)  95.9 us
    all_gather x1, waiting for transfers between devices, body(): compact = lax.all_gather(panels, 'pr', axis=1, tiled=True)  43.8 us
    dot_general x1, matrix products, body(): jnp.einsum('ji,cjn->cin', root_inverse, lax.all_gather(expanded, 'pc', ax...  17.2 us
  transfers between devices with their start and end apart: 4, of which 4 were waited for; matrix products, arithmetic and copies ran while one was open for 0% of the time, Pallas kernels for 0%

commit v1 on v0

v1 whole, which is shorter than its diff:
```python
import jax
import jax.numpy as jnp
from jax import lax
from jax.experimental import pallas as pl
from jax.experimental.pallas import tpu as pltpu
from jax.sharding import PartitionSpec as P

BLOCK = 256
MESH = pl.DeviceIdType.MESH
F32 = jnp.float32
BF16 = jnp.bfloat16


def split(value):
    high = value.astype(BF16)
    low = (value - high.astype(F32)).astype(BF16)
    return high, low


def kernel(
    rows_ref, a_ref, p_ref, b_ref, c_out, d_out,
    a1, a2s, a2r, acat, pg, pcat, w, sr, x1, x2, zs, zr,
    c1a, c1b, c2s, c2r, ccat, tw, tr, ts, tf,
    a1_send, a1_recv, a2_send, a2_recv, pz_send, pz_recv, py_send, py_recv,
    sib_send, sib_recv, x1_send, x1_recv, x2_send, x2_recv, z_send, z_recv,
    c1_send, c1_recv, c2_send, c2_recv, tr_send, tr_recv, tf_send, tf_recv,
):
    r = lax.axis_index("pr")
    c = lax.axis_index("pc")
    x, zl, co = r // 4, (r // 2) % 2, r % 2
    y, zh = c // 4, c % 4

    def chip(xx, zz, cc):
        return (xx * 4 + zz * 2 + cc, c)

    c1 = (c1a, c1b)
    sibling = chip(x, zl, 1 - co)
    zpartner = chip(x, 1 - zl, co)
    xright = chip((x + 1) % 4, zl, co)
    xleft = chip((x + 3) % 4, zl, co)

    def remote(src, dst, send, recv, device):
        return pltpu.make_async_remote_copy(
            src_ref=src, dst_ref=dst, send_sem=send, recv_sem=recv,
            device_id=device, device_id_type=MESH,
        )

    def wait_bytes(ref, sem):
        pltpu.make_async_copy(ref, ref, sem).wait()

    barrier = pltpu.get_barrier_semaphore()

    def greet(k, carry):
        pl.semaphore_signal(barrier, inc=1, device_id=((r + k) % 16, c), device_id_type=MESH)
        pl.semaphore_signal(barrier, inc=1, device_id=(r, (c + k) % 16), device_id_type=MESH)
        return carry

    lax.fori_loop(1, 16, greet, 0)

    def greet_senders(k, carry):
        @pl.when((r != c) | (k != c))
        def _():
            pl.semaphore_signal(barrier, inc=1, device_id=(c, k), device_id_type=MESH)

        return carry

    lax.fori_loop(0, 16, greet_senders, 0)

    @pl.when(r == c)
    def _():
        pl.semaphore_wait(barrier, 45)

    @pl.when(r != c)
    def _():
        pl.semaphore_wait(barrier, 46)

    def a_spread(k, carry):
        to = (r + k) % 16
        remote(
            a_ref.at[:, pl.ds(to * 16, 16), :], a1.at[pl.ds(r * 2, 2)],
            a1_send, a1_recv, (to, c),
        ).start()
        return carry

    lax.fori_loop(1, 16, a_spread, 0)

    def p_own(child):
        def along_z(k, carry):
            remote(
                p_ref.at[child], pg.at[c, child], pz_send.at[child],
                pz_recv.at[child, k - 1], (r, y * 4 + (zh + k) % 4),
            ).start()
            return carry

        def along_y(k, carry):
            remote(
                p_ref.at[child], pg.at[c, child], py_send.at[child],
                py_recv.at[child], (r, ((y + k) % 4) * 4 + zh),
            ).start()
            return carry

        lax.fori_loop(1, 4, along_z, 0)
        lax.fori_loop(1, 4, along_y, 0)

    def p_forward(child):
        def piece(k, carry):
            source = y * 4 + (zh + 4 - k) % 4
            wait_bytes(pg.at[source, child], pz_recv.at[child, k - 1])

            def along_y(j, inner):
                remote(
                    pg.at[source, child], pg.at[source, child], py_send.at[child],
                    py_recv.at[child], (r, ((y + j) % 4) * 4 + zh),
                ).start()
                return inner

            lax.fori_loop(1, 4, along_y, 0)
            return carry

        lax.fori_loop(1, 4, piece, 0)

    p_own(0)
    a1[pl.ds(r * 2, 2)] = a_ref[:, pl.ds(r * 16, 16), :]
    pg[c] = p_ref[...]
    wait_bytes(a1.at[pl.ds(0, 30)], a1_recv)

    def a_list(child):
        def place(t, carry):
            a2s[child, t] = -a1[rows_ref[child, t]]
            return carry

        lax.fori_loop(0, 16, place, 0)

        def deal(k, carry):
            to = (r + k) % 16
            remote(
                a2s.at[child, to], a2r.at[child, pl.ds(r * 16, 16), :],
                a2_send.at[child], a2_recv.at[child], (to, c),
            ).start()
            return carry

        lax.fori_loop(1, 16, deal, 0)
        a2r[child, pl.ds(r * 16, 16), :] = a2s[child, r]

    a_list(0)
    p_forward(0)
    a_list(1)
    p_own(1)
    p_forward(1)

    def prepare(child):
        wait_bytes(a2r.at[child, pl.ds(0, 240), :], a2_recv.at[child])
        high, low = split(a2r[child].T)
        acat[child, :, 0:256] = high
        acat[child, :, 256:512] = high
        acat[child, :, 512:768] = low
        wait_bytes(pg.at[pl.ds(0, 12), child], py_recv.at[child])

        def pair(q, carry):
            for half in range(2):
                lanes = pl.ds(half * 128, 128)
                high, low = split(pg[q * 2 + half, child])
                pcat[child, q, 0:256, lanes] = high
                pcat[child, q, 256:512, lanes] = low
                pcat[child, q, 512:768, lanes] = high
            return carry

        lax.fori_loop(0, 8, pair, 0)

    def layer(item):
        return 1 - zl if item % 2 == 0 else zl

    def products(item):
        child = item // 2

        def one(j, carry):
            q = ((x + 6 - j) % 4) * 2 + layer(item)
            result = jnp.dot(acat[child], pcat[child, q], preferred_element_type=F32)
            w[item, j, 0] = result[:, 0:128]
            w[item, j, 1] = result[:, 128:256]
            remote(
                w.at[item, j, 1 - co], sr.at[item, j], sib_send.at[item, j],
                sib_recv.at[item, j], sibling,
            ).start()
            return carry

        lax.fori_loop(0, 4, one, 0)

    def chip_sum(item, j):
        wait_bytes(sr.at[item, j], sib_recv.at[item, j])
        sr[item, j] = sr[item, j] + w[item, j, co]

    def x_first(item):
        chip_sum(item, 0)
        remote(
            sr.at[item, 0, pl.ds(0, 256), :], x1.at[item, 0], x1_send.at[item, 0],
            x1_recv.at[item, 0], xright,
        ).start()
        remote(
            sr.at[item, 0, pl.ds(256, 256), :], x1.at[item, 1], x1_send.at[item, 1],
            x1_recv.at[item, 1], xleft,
        ).start()

    def x_second(item):
        chip_sum(item, 1)
        wait_bytes(x1.at[item, 0], x1_recv.at[item, 0])
        sr[item, 1, 0:256, :] = sr[item, 1, 0:256, :] + x1[item, 0]
        remote(
            sr.at[item, 1], x2.at[item, 0], x2_send.at[item, 0],
            x2_recv.at[item, 0], xright,
        ).start()
        chip_sum(item, 3)
        wait_bytes(x1.at[item, 1], x1_recv.at[item, 1])
        sr[item, 3, 256:512, :] = sr[item, 3, 256:512, :] + x1[item, 1]
        remote(
            sr.at[item, 3], x2.at[item, 1], x2_send.at[item, 1],
            x2_recv.at[item, 1], xleft,
        ).start()

    def x_last(item):
        child = item // 2
        chip_sum(item, 2)
        wait_bytes(x2.at[item, 0], x2_recv.at[item, 0])
        wait_bytes(x2.at[item, 1], x2_recv.at[item, 1])
        total = sr[item, 2] + x2[item, 0] + x2[item, 1]
        if item % 2 == 0:
            zs[child] = total
            remote(
                zs.at[child], zr.at[child], z_send.at[child], z_recv.at[child], zpartner
            ).start()
        else:
            wait_bytes(zr.at[child], z_recv.at[child])
            c_out[child] = (total + zr[child]).reshape(2, BLOCK, 128)

    def c_spread(child):
        def one(k, carry):
            to = (c + k) % 16
            remote(
                c_out.at[child, :, pl.ds(to * 16, 16), :], c1[child].at[pl.ds(c * 2, 2)],
                c1_send.at[child], c1_recv.at[child], (r, to),
            ).start()
            return carry

        lax.fori_loop(1, 16, one, 0)
        c1[child][pl.ds(c * 2, 2)] = c_out[child, :, pl.ds(c * 16, 16), :]

    def c_list(child):
        wait_bytes(c1[child].at[pl.ds(0, 30)], c1_recv.at[child])

        def place(t, carry):
            c2s[child, t] = c1[child][rows_ref[child, t]]
            return carry

        lax.fori_loop(0, 16, place, 0)

        def deal(t, carry):
            source = c2s.at[child, t]
            target = c2r.at[child, pl.ds(c * 16, 16), :]

            @pl.when((r != c) | (t != r))
            def _():
                remote(source, target, c2_send.at[child], c2_recv.at[child], (t, r)).start()

            return carry

        lax.fori_loop(0, 16, deal, 0)

        @pl.when(r == c)
        def _():
            c2r[child, pl.ds(c * 16, 16), :] = c2s[child, r]

    def terms(child):
        @pl.when(r == c)
        def _():
            wait_bytes(c2r.at[child, pl.ds(0, 240), :], c2_recv.at[child])

        @pl.when(r != c)
        def _():
            wait_bytes(c2r.at[child], c2_recv.at[child])

        high, low = split(c2r[child].T)
        ccat[child, :, 0:256] = high
        ccat[child, :, 256:512] = high
        ccat[child, :, 512:768] = low

        def one(q, carry):
            result = jnp.dot(ccat[child], pcat[child, q], preferred_element_type=F32)
            tw[child, 0, q] = result[:, 0:128]
            tw[child, 1, q] = result[:, 128:256]
            return carry

        lax.fori_loop(0, 8, one, 0)
        remote(
            tw.at[child, 1 - co], tr.at[child], tr_send.at[child], tr_recv.at[child], sibling
        ).start()

    def terms_spread(child):
        wait_bytes(tr.at[child], tr_recv.at[child])
        ts[child] = tw[child, co] + tr[child]
        mine = r // 2

        def one(k, carry):
            to = (mine + k) % 8
            remote(
                ts.at[child, to], tf.at[child, mine], tf_send.at[child],
                tf_recv.at[child], (to * 2 + co, c),
            ).start()
            return carry

        lax.fori_loop(1, 8, one, 0)
        tf[child, mine] = ts[child, mine]

    def diagonal(child):
        wait_bytes(tf.at[child, pl.ds(0, 7)], tf_recv.at[child])
        total = tf[child, 0]
        for k in range(1, 8):
            total = total + tf[child, k]
        d_out[child] = b_ref[child] - total

    prepare(0)
    products(0)
    x_first(0)
    products(1)
    x_first(1)
    x_second(0)
    x_second(1)
    prepare(1)
    products(2)
    x_first(2)
    x_last(0)
    products(3)
    x_first(3)
    x_second(2)
    x_last(1)
    c_spread(0)
    x_second(3)
    c_list(0)
    x_last(2)
    terms(0)
    x_last(3)
    c_spread(1)
    terms_spread(0)
    c_list(1)
    terms(1)
    diagonal(0)
    terms_spread(1)
    diagonal(1)

    wait_bytes(a1.at[pl.ds(0, 30)], a1_send)
    for child in range(2):
        wait_bytes(a2r.at[child, pl.ds(0, 240), :], a2_send.at[child])
        wait_bytes(pg.at[pl.ds(0, 3), child], pz_send.at[child])
        wait_bytes(pg.at[pl.ds(0, 12), child], py_send.at[child])
        wait_bytes(zs.at[child], z_send.at[child])
        wait_bytes(c1[child].at[pl.ds(0, 30)], c1_send.at[child])

        @pl.when(r == c)
        def _():
            wait_bytes(c2r.at[child, pl.ds(0, 240), :], c2_send.at[child])

        @pl.when(r != c)
        def _():
            wait_bytes(c2r.at[child], c2_send.at[child])

        wait_bytes(tr.at[child], tr_send.at[child])
        wait_bytes(tf.at[child, pl.ds(0, 7)], tf_send.at[child])
    for item in range(4):
        for j in range(4):
            wait_bytes(sr.at[item, j], sib_send.at[item, j])
        for side in range(2):
            wait_bytes(x1.at[item, side], x1_send.at[item, side])
            wait_bytes(x2.at[item, side], x2_send.at[item, side])


def body(root_inverse, panels, child_rows, block_inverse):
    vmem = pl.BlockSpec(memory_space=pltpu.VMEM)
    dma = pltpu.SemaphoreType.DMA
    coupling, diagonal = pl.pallas_call(
        kernel,
        out_shape=(
            jax.ShapeDtypeStruct((2, 2, BLOCK, 128), F32),
            jax.ShapeDtypeStruct((2, 128, 128), F32),
        ),
        in_specs=[pl.BlockSpec(memory_space=pltpu.SMEM), vmem, vmem, vmem],
        out_specs=(vmem, vmem),
        scratch_shapes=[
            pltpu.VMEM((32, 16, 512), F32),
            pltpu.VMEM((2, 16, 16, 512), F32),
            pltpu.VMEM((2, 256, 512), F32),
            pltpu.VMEM((2, 512, 768), BF16),
            pltpu.VMEM((16, 2, 256, 128), F32),
            pltpu.VMEM((2, 8, 768, 256), BF16),
            pltpu.VMEM((4, 4, 2, 512, 128), F32),
            pltpu.VMEM((4, 4, 512, 128), F32),
            pltpu.VMEM((4, 2, 256, 128), F32),
            pltpu.VMEM((4, 2, 512, 128), F32),
            pltpu.VMEM((2, 512, 128), F32),
            pltpu.VMEM((2, 512, 128), F32),
            pltpu.VMEM((32, 16, 128), F32),
            pltpu.VMEM((32, 16, 128), F32),
            pltpu.VMEM((2, 16, 16, 128), F32),
            pltpu.VMEM((2, 256, 128), F32),
            pltpu.VMEM((2, 128, 768), BF16),
            pltpu.VMEM((2, 2, 8, 128, 128), F32),
            pltpu.VMEM((2, 8, 128, 128), F32),
            pltpu.VMEM((2, 8, 128, 128), F32),
            pltpu.VMEM((2, 8, 128, 128), F32),
            dma, dma,
            dma((2,)), dma((2,)),
            dma((2,)), dma((2, 3)),
            dma((2,)), dma((2,)),
            dma((4, 4)), dma((4, 4)),
            dma((4, 2)), dma((4, 2)),
            dma((4, 2)), dma((4, 2)),
            dma((2,)), dma((2,)),
            dma((2,)), dma((2,)),
            dma((2,)), dma((2,)),
            dma((2,)), dma((2,)),
            dma((2,)), dma((2,)),
        ],
        compiler_params=pltpu.CompilerParams(
            collective_id=0, has_side_effects=True, vmem_limit_bytes=52 * 1024 * 1024
        ),
        cost_estimate=pl.CostEstimate(
            flops=3 * 2 * 2 * 256 * 2048 * (512 + 128), bytes_accessed=4 << 20, transcendentals=0
        ),
    )(child_rows, root_inverse.reshape(2, BLOCK, 512), panels, block_inverse)
    return coupling.reshape(2, 2 * BLOCK, 128), diagonal


def solution(mesh):
    in_specs = (P("pr", "pc"), P(None, "pr", "pc"), P(), P(None, "pc", "pr"))
    out_specs = (P(None, "pc", "pr"), P(None, "pc", "pr"))
    return jax.shard_map(body, mesh=mesh, in_specs=in_specs, out_specs=out_specs, check_vma=False)
```

time: 560 us -> 141 us (0.25)
  the two profiles are of different devices: /device:TPU:35 before, /device:TPU:1 now
where the time goes in v1:
time: 141 us
  Pallas kernels  137 us (97%)
  local copies, waits for them, and re-layouts  3.98 us (3%)
    pallas_call x1, Pallas kernels, body(): pl.pallas_call(kernel, out_shape=(jax.ShapeDtypeStruct((2, 2, BLOCK, 128)...  137 us
    unnamed x8, local copies, waits for them, and re-layouts  3.98 us

profile of v1, /device:TPU:1, one launch (start us, length us, event | category | flops | bytes accessed | tf_op | source)
XLA Modules:
  0.0 141.3 jit_solution(9829823098077148243)
XLA Ops:
  0.6 0.0 copy-start.2
  0.6 0.7 copy-done.2
  1.3 0.0 copy-start
  1.3 0.9 copy-done
  2.3 0.0 copy-start.1
  2.3 0.9 copy-done.1
  3.2 136.6 %shard_map.59 = (f32[2,2,256,128]{3,2,1,0:T(8,128)S(1)}, f32[2,128,128]{2,1,0:T(8,128)S(1)}) custom-call(s32[2,16]{1,0:T(2,128)S(1)} %copy-done.2, f32[2,256,512]{2,1,0:T(8,128)} %bitcast.3, f32[2,256,128]{2,1,0:T(8,128)S(1)} %copy-done, f32[2,128,128]{2,1,0:T(8,128)S(1)} %copy-done.1), custom_call_target="tpu_custom_call" | custom-call | flops 4026531840 | bytes 4194304 | tf_op jit(solution)/shard_map/pallas_call | solution.py:378
  139.8 0.8 copy.8
  140.6 0.7 copy.9
Async XLA Ops:
  0.6 0.7 copy-start.2
  1.3 0.9 copy-start
  2.3 0.9 copy-start.1

commit v2 on v1

v2 whole, which is shorter than its diff:
```python
import jax
import jax.numpy as jnp
from jax import lax
from jax.experimental import pallas as pl
from jax.experimental.pallas import tpu as pltpu
from jax.sharding import PartitionSpec as P

BLOCK = 256
MESH = pl.DeviceIdType.MESH
F32 = jnp.float32
BF16 = jnp.bfloat16


def split(value):
    high = value.astype(BF16)
    low = (value - high.astype(F32)).astype(BF16)
    return high, low


def kernel(
    rows_ref, a_ref, p_ref, b_ref, c_out, d_out,
    a1, a2, acat, pg, pcat, w, sr, x1, x2, zs, zr,
    c1a, c1b, c2, ccat, tw, tr, ts, tf,
    own_sem, a1_send, a1_recv, pa_send, pa_recv, pz_send, pz_recv, pzh_recv,
    py_send, py_recv, pyh_recv,
    sib_send, sib_recv, x1_send, x1_recv, x2_send, x2_recv, z_send, z_recv,
    c1_send, c1_recv, tr_send, tr_recv, tf_send, tf_recv,
):
    r = lax.axis_index("pr")
    c = lax.axis_index("pc")
    x, zl, co = r // 4, (r // 2) % 2, r % 2
    y, zh = c // 4, c % 4

    def chip(xx, zz, cc):
        return (xx * 4 + zz * 2 + cc, c)

    c1 = (c1a, c1b)
    zup, zdown = y * 4 + (zh + 1) % 4, y * 4 + (zh + 3) % 4
    yup, ydown = ((y + 1) % 4) * 4 + zh, ((y + 3) % 4) * 4 + zh
    places = (zh, (zh + 3) % 4, (zh + 1) % 4, (zh + 2) % 4)
    low_half, high_half = pl.ds(0, 128), pl.ds(128, 128)
    sibling = chip(x, zl, 1 - co)
    zpartner = chip(x, 1 - zl, co)
    xright = chip((x + 1) % 4, zl, co)
    xleft = chip((x + 3) % 4, zl, co)

    def remote(src, dst, send, recv, device):
        return pltpu.make_async_remote_copy(
            src_ref=src, dst_ref=dst, send_sem=send, recv_sem=recv,
            device_id=device, device_id_type=MESH,
        )

    def wait_bytes(ref, sem):
        pltpu.make_async_copy(ref, ref, sem).wait()

    barrier = pltpu.get_barrier_semaphore()

    def greet(k, carry):
        pl.semaphore_signal(barrier, inc=1, device_id=((r + k) % 16, c), device_id_type=MESH)
        return carry

    lax.fori_loop(1, 16, greet, 0)
    for plane in (zup, zdown, yup, ydown):
        pl.semaphore_signal(barrier, inc=1, device_id=(r, plane), device_id_type=MESH)

    def greet_senders(k, carry):
        @pl.when((r != c) | (k != c))
        def _():
            pl.semaphore_signal(barrier, inc=1, device_id=(c, k), device_id_type=MESH)

        return carry

    lax.fori_loop(0, 16, greet_senders, 0)

    @pl.when(r == c)
    def _():
        pl.semaphore_wait(barrier, 34)

    @pl.when(r != c)
    def _():
        pl.semaphore_wait(barrier, 35)

    def a_spread():
        lax.fori_loop(1, 16, a_spread_one, 0)

    def a_spread_one(k, carry):
        to = (r + k) % 16
        remote(
            a_ref.at[:, pl.ds(to * 16, 16), :], a1.at[pl.ds(r * 2, 2)],
            a1_send, a1_recv, (to, c),
        ).start()
        return carry


    def p_spread(child):
        def one(k, carry):
            to = (r + k) % 16
            remote(
                p_ref.at[child, pl.ds(to * 16, 16), :], pg.at[c, child, pl.ds(r * 16, 16), :],
                pa_send.at[child], pa_recv.at[child], (to, c),
            ).start()
            return carry

        lax.fori_loop(1, 16, one, 0)

    def p_gathered(child):
        wait_bytes(pg.at[c, child, pl.ds(0, 240), :], pa_recv.at[child])

    def send_piece(piece, child, to, send, recv):
        remote(pg.at[piece, child], pg.at[piece, child], send, recv, (r, to)).start()

    def send_half(piece, child, half, to, send, recv):
        ref = pg.at[piece, child, half, :]
        remote(ref, ref, send, recv, (r, to)).start()

    def p_z(child):
        send_piece(c, child, zup, pz_send.at[child], pz_recv.at[child, 0])
        send_piece(c, child, zdown, pz_send.at[child], pz_recv.at[child, 1])

    def p_y(child, k):
        piece = y * 4 + places[k]
        send_piece(piece, child, yup, py_send.at[child], py_recv.at[child, k, 0])
        send_piece(piece, child, ydown, py_send.at[child], py_recv.at[child, k, 1])

    def p_z_pass(child):
        wait_bytes(pg.at[zdown, child], pz_recv.at[child, 0])
        send_half(zdown, child, low_half, zup, pz_send.at[child], pzh_recv.at[child, 0])
        wait_bytes(pg.at[zup, child], pz_recv.at[child, 1])
        send_half(zup, child, high_half, zdown, pz_send.at[child], pzh_recv.at[child, 1])

    def p_z_last(child):
        piece = y * 4 + places[3]
        wait_bytes(pg.at[piece, child, low_half, :], pzh_recv.at[child, 0])
        wait_bytes(pg.at[piece, child, high_half, :], pzh_recv.at[child, 1])

    def p_y_pass(child, k):
        below, above = ((y + 3) % 4) * 4 + places[k], ((y + 1) % 4) * 4 + places[k]
        wait_bytes(pg.at[below, child], py_recv.at[child, k, 0])
        send_half(below, child, low_half, yup, py_send.at[child], pyh_recv.at[child, k, 0])
        wait_bytes(pg.at[above, child], py_recv.at[child, k, 1])
        send_half(above, child, high_half, ydown, py_send.at[child], pyh_recv.at[child, k, 1])

    def p_y_last(child, k):
        piece = ((y + 2) % 4) * 4 + places[k]
        wait_bytes(pg.at[piece, child, low_half, :], pyh_recv.at[child, k, 0])
        wait_bytes(pg.at[piece, child, high_half, :], pyh_recv.at[child, k, 1])

    a_own = pltpu.make_async_copy(
        a_ref.at[:, pl.ds(r * 16, 16), :], a1.at[pl.ds(r * 2, 2)], own_sem.at[0]
    )
    p_mine = [
        pltpu.make_async_copy(
            p_ref.at[child, pl.ds(r * 16, 16), :], pg.at[c, child, pl.ds(r * 16, 16), :],
            own_sem.at[1 + child],
        )
        for child in range(2)
    ]

    def own():
        for copy in (p_mine[0], p_mine[1], a_own):
            copy.start()

    def own_ready():
        for copy in (p_mine[0], p_mine[1], a_own):
            copy.wait()

    def a_gathered():
        wait_bytes(a1.at[pl.ds(0, 30)], a1_recv)

    def a_list(child):
        for t in range(16):
            a2[child, t * 16:(t + 1) * 16, :] = -a1[rows_ref[child, t]]
        high, low = split(a2[child].T)
        acat[child, :, 0:256] = high
        acat[child, :, 256:512] = high
        acat[child, :, 512:768] = low

    def p_ready(child):
        for k in range(4):
            p_y_last(child, k)

        def pair(q, carry):
            for half in range(2):
                lanes = pl.ds(half * 128, 128)
                high, low = split(pg[q * 2 + half, child])
                pcat[child, q, 0:256, lanes] = high
                pcat[child, q, 256:512, lanes] = low
                pcat[child, q, 512:768, lanes] = high
            return carry

        lax.fori_loop(0, 8, pair, 0)

    def layer(item):
        return 1 - zl if item % 2 == 0 else zl

    def products(item):
        child = item // 2

        def one(j, carry):
            q = ((x + 6 - j) % 4) * 2 + layer(item)
            result = jnp.dot(acat[child], pcat[child, q], preferred_element_type=F32)
            w[item, j, 0] = result[:, 0:128]
            w[item, j, 1] = result[:, 128:256]
            remote(
                w.at[item, j, 1 - co], sr.at[item, j], sib_send.at[item, j],
                sib_recv.at[item, j], sibling,
            ).start()
            return carry

        lax.fori_loop(0, 4, one, 0)

    def chip_sum(item, j):
        wait_bytes(sr.at[item, j], sib_recv.at[item, j])
        sr[item, j] = sr[item, j] + w[item, j, co]

    def x_first(item):
        chip_sum(item, 0)
        remote(
            sr.at[item, 0, pl.ds(0, 256), :], x1.at[item, 0], x1_send.at[item, 0],
            x1_recv.at[item, 0], xright,
        ).start()
        remote(
            sr.at[item, 0, pl.ds(256, 256), :], x1.at[item, 1], x1_send.at[item, 1],
            x1_recv.at[item, 1], xleft,
        ).start()

    def x_second(item):
        chip_sum(item, 1)
        wait_bytes(x1.at[item, 0], x1_recv.at[item, 0])
        sr[item, 1, 0:256, :] = sr[item, 1, 0:256, :] + x1[item, 0]
        remote(
            sr.at[item, 1], x2.at[item, 0], x2_send.at[item, 0],
            x2_recv.at[item, 0], xright,
        ).start()
        chip_sum(item, 3)
        wait_bytes(x1.at[item, 1], x1_recv.at[item, 1])
        sr[item, 3, 256:512, :] = sr[item, 3, 256:512, :] + x1[item, 1]
        remote(
            sr.at[item, 3], x2.at[item, 1], x2_send.at[item, 1],
            x2_recv.at[item, 1], xleft,
        ).start()

    def x_last(item):
        child = item // 2
        chip_sum(item, 2)
        wait_bytes(x2.at[item, 0], x2_recv.at[item, 0])
        wait_bytes(x2.at[item, 1], x2_recv.at[item, 1])
        total = sr[item, 2] + x2[item, 0] + x2[item, 1]
        if item % 2 == 0:
            zs[child] = total
            remote(
                zs.at[child], zr.at[child], z_send.at[child], z_recv.at[child], zpartner
            ).start()
        else:
            wait_bytes(zr.at[child], z_recv.at[child])
            c_out[child] = (total + zr[child]).reshape(2, BLOCK, 128)

    def c_spread(child):
        def one(u, carry):
            source = c_out.at[child, :, pl.ds(u * 16, 16), :]
            target = c1[child].at[pl.ds(c * 2, 2)]

            @pl.when((r != c) | (u != r))
            def _():
                remote(source, target, c1_send.at[child], c1_recv.at[child], (u, r)).start()

            return carry

        lax.fori_loop(0, 16, one, 0)

        @pl.when(r == c)
        def _():
            c1[child][pl.ds(c * 2, 2)] = c_out[child, :, pl.ds(r * 16, 16), :]

    def c_wait(child, sem):
        @pl.when(r == c)
        def _():
            wait_bytes(c1[child].at[pl.ds(0, 30)], sem)

        @pl.when(r != c)
        def _():
            wait_bytes(c1[child], sem)

    def c_ready(child):
        c_wait(child, c1_recv.at[child])
        for t in range(16):
            c2[child, t * 16:(t + 1) * 16, :] = c1[child][rows_ref[child, t]]

    def terms(child):
        high, low = split(c2[child].T)
        ccat[child, :, 0:256] = high
        ccat[child, :, 256:512] = high
        ccat[child, :, 512:768] = low

        def one(q, carry):
            result = jnp.dot(ccat[child], pcat[child, q], preferred_element_type=F32)
            tw[child, 0, q] = result[:, 0:128]
            tw[child, 1, q] = result[:, 128:256]
            return carry

        lax.fori_loop(0, 8, one, 0)
        remote(
            tw.at[child, 1 - co], tr.at[child], tr_send.at[child], tr_recv.at[child], sibling
        ).start()

    def terms_spread(child):
        wait_bytes(tr.at[child], tr_recv.at[child])
        ts[child] = tw[child, co] + tr[child]
        mine = r // 2

        def one(k, carry):
            to = (mine + k) % 8
            remote(
                ts.at[child, to], tf.at[child, mine], tf_send.at[child],
                tf_recv.at[child], (to * 2 + co, c),
            ).start()
            return carry

        lax.fori_loop(1, 8, one, 0)
        tf[child, mine] = ts[child, mine]

    def diagonal(child):
        wait_bytes(tf.at[child, pl.ds(0, 7)], tf_recv.at[child])
        total = tf[child, 0]
        for k in range(1, 8):
            total = total + tf[child, k]
        d_out[child] = b_ref[child] - total

    def a_sent():
        wait_bytes(a1.at[pl.ds(0, 30)], a1_send)

    def p_sent(child):
        wait_bytes(pg.at[c, child, pl.ds(0, 240), :], pa_send.at[child])
        wait_bytes(pg.at[pl.ds(0, 3), child], pz_send.at[child])
        wait_bytes(pg.at[pl.ds(0, 12), child], py_send.at[child])

    def r_sent(child):
        wait_bytes(zs.at[child], z_send.at[child])
        for item in (2 * child, 2 * child + 1):
            for j in range(4):
                wait_bytes(sr.at[item, j], sib_send.at[item, j])
            for side in range(2):
                wait_bytes(x1.at[item, side], x1_send.at[item, side])
                wait_bytes(x2.at[item, side], x2_send.at[item, side])

    def c_sent(child):
        c_wait(child, c1_send.at[child])

    def t_sent(child):
        wait_bytes(tr.at[child], tr_send.at[child])
        wait_bytes(tf.at[child, pl.ds(0, 7)], tf_send.at[child])

    own()
    p_spread(0)
    p_spread(1)
    own_ready()
    p_gathered(0)
    p_z(0)
    p_y(0, 0)
    p_gathered(1)
    p_z(1)
    p_y_pass(0, 0)
    p_z_pass(0)
    a_spread()
    p_y(0, 1)
    p_y(0, 2)
    p_z_last(0)
    p_y(0, 3)
    p_y_pass(0, 1)
    p_y_pass(0, 2)
    p_y_pass(0, 3)
    p_y(1, 0)
    a_gathered()
    a_list(0)
    a_list(1)
    p_ready(0)
    products(0)
    x_first(0)
    p_z_pass(1)
    p_y(1, 1)
    p_y(1, 2)
    products(1)
    x_first(1)
    p_z_last(1)
    p_y(1, 3)
    p_y_pass(1, 0)
    x_second(0)
    p_y_pass(1, 1)
    p_y_pass(1, 2)
    x_second(1)
    x_last(0)
    p_y_pass(1, 3)
    x_last(1)
    c_spread(0)
    p_ready(1)
    products(2)
    x_first(2)
    products(3)
    x_first(3)
    x_second(2)
    c_ready(0)
    x_second(3)
    terms(0)
    x_last(2)
    terms_spread(0)
    x_last(3)
    c_spread(1)
    diagonal(0)
    c_ready(1)
    terms(1)
    terms_spread(1)
    diagonal(1)

    a_sent()
    for child in range(2):
        p_sent(child)
        r_sent(child)
        c_sent(child)
        t_sent(child)


def body(root_inverse, panels, child_rows, block_inverse):
    vmem = pl.BlockSpec(memory_space=pltpu.VMEM)
    hbm = pl.BlockSpec(memory_space=pl.ANY)
    dma = pltpu.SemaphoreType.DMA
    coupling, diagonal = pl.pallas_call(
        kernel,
        out_shape=(
            jax.ShapeDtypeStruct((2, 2, BLOCK, 128), F32),
            jax.ShapeDtypeStruct((2, 128, 128), F32),
        ),
        in_specs=[pl.BlockSpec(memory_space=pltpu.SMEM), hbm, hbm, vmem],
        out_specs=(vmem, vmem),
        scratch_shapes=[
            pltpu.VMEM((32, 16, 512), F32),
            pltpu.VMEM((2, 256, 512), F32),
            pltpu.VMEM((2, 512, 768), BF16),
            pltpu.VMEM((16, 2, 256, 128), F32),
            pltpu.VMEM((2, 8, 768, 256), BF16),
            pltpu.VMEM((4, 4, 2, 512, 128), F32),
            pltpu.VMEM((4, 4, 512, 128), F32),
            pltpu.VMEM((4, 2, 256, 128), F32),
            pltpu.VMEM((4, 2, 512, 128), F32),
            pltpu.VMEM((2, 512, 128), F32),
            pltpu.VMEM((2, 512, 128), F32),
            pltpu.VMEM((32, 16, 128), F32),
            pltpu.VMEM((32, 16, 128), F32),
            pltpu.VMEM((2, 256, 128), F32),
            pltpu.VMEM((2, 128, 768), BF16),
            pltpu.VMEM((2, 2, 8, 128, 128), F32),
            pltpu.VMEM((2, 8, 128, 128), F32),
            pltpu.VMEM((2, 8, 128, 128), F32),
            pltpu.VMEM((2, 8, 128, 128), F32),
            dma((3,)),
            dma, dma,
            dma((2,)), dma((2,)),
            dma((2,)), dma((2, 2)), dma((2, 2)),
            dma((2,)), dma((2, 4, 2)), dma((2, 4, 2)),
            dma((4, 4)), dma((4, 4)),
            dma((4, 2)), dma((4, 2)),
            dma((4, 2)), dma((4, 2)),
            dma((2,)), dma((2,)),
            dma((2,)), dma((2,)),
            dma((2,)), dma((2,)),
            dma((2,)), dma((2,)),
        ],
        compiler_params=pltpu.CompilerParams(
            collective_id=0, has_side_effects=True, vmem_limit_bytes=52 * 1024 * 1024
        ),
        cost_estimate=pl.CostEstimate(
            flops=3 * 2 * 2 * 256 * 2048 * (512 + 128), bytes_accessed=4 << 20, transcendentals=0
        ),
    )(child_rows, root_inverse.reshape(2, BLOCK, 512), panels, block_inverse)
    return coupling.reshape(2, 2 * BLOCK, 128), diagonal


def solution(mesh):
    in_specs = (P("pr", "pc"), P(None, "pr", "pc"), P(), P(None, "pc", "pr"))
    out_specs = (P(None, "pc", "pr"), P(None, "pc", "pr"))
    return jax.shard_map(body, mesh=mesh, in_specs=in_specs, out_specs=out_specs, check_vma=False)
```

time: 141 us -> 125 us (0.89)
  Pallas kernels: 137 us -> 120 us
    pallas_call x1, Pallas kernels: 137 us -> 120 us  [body(): pl.pallas_call(kernel, out_shape=(jax.ShapeDtypeStruct((2, 2, BLOCK, 128)...]
where the time goes in v2:
time: 125 us
  Pallas kernels  120 us (96%)
  local copies, waits for them, and re-layouts  3.98 us (3%)
    pallas_call x1, Pallas kernels, body(): pl.pallas_call(kernel, out_shape=(jax.ShapeDtypeStruct((2, 2, BLOCK, 128)...  120 us
    unnamed x8, local copies, waits for them, and re-layouts  3.98 us

profile of v2, /device:TPU:1, one launch (start us, length us, event | category | flops | bytes accessed | tf_op | source)
XLA Modules:
  0.0 125.1 jit_solution(14930287096743855866)
XLA Ops:
  0.6 0.0 copy-start.2
  0.6 0.7 copy-done.2
  1.3 0.0 copy-start
  1.3 0.9 copy-done
  2.3 0.0 copy-start.1
  2.3 0.9 copy-done.1
  3.2 120.5 %shard_map.59 = (f32[2,2,256,128]{3,2,1,0:T(8,128)S(1)}, f32[2,128,128]{2,1,0:T(8,128)S(1)}) custom-call(s32[2,16]{1,0:T(2,128)S(1)} %copy-done.2, f32[2,256,512]{2,1,0:T(8,128)} %bitcast.3, f32[2,256,128]{2,1,0:T(8,128)S(1)} %copy-done, f32[2,128,128]{2,1,0:T(8,128)S(1)} %copy-done.1), custom_call_target="tpu_custom_call" | custom-call | flops 4026531840 | bytes 4194304 | tf_op jit(solution)/shard_map/pallas_call | solution.py:426
  123.7 0.8 copy.8
  124.5 0.7 copy.9
Async XLA Ops:
  0.6 0.7 copy-start.2
  1.3 0.9 copy-start
  2.3 0.9 copy-start.1

commit v3 on v2

--- a/solution.py
+++ b/solution.py
@@ -19,11 +19,11 @@
 
 def kernel(
     rows_ref, a_ref, p_ref, b_ref, c_out, d_out,
-    a1, a2, acat, pg, pcat, w, sr, x1, x2, zs, zr,
+    a1, a2, acat, pg, pcat, w, sr, x1, x2, zs, zr, zq,
     c1a, c1b, c2, ccat, tw, tr, ts, tf,
     own_sem, a1_send, a1_recv, pa_send, pa_recv, pz_send, pz_recv, pzh_recv,
     py_send, py_recv, pyh_recv,
-    sib_send, sib_recv, x1_send, x1_recv, x2_send, x2_recv, z_send, z_recv,
+    sib_send, sib_recv, x1_send, x1_recv, x2_send, x2_recv, z_send, z_recv, zq_send, zq_recv,
     c1_send, c1_recv, tr_send, tr_recv, tf_send, tf_recv,
 ):
     r = lax.axis_index("pr")
@@ -190,75 +190,80 @@
 
         lax.fori_loop(0, 8, pair, 0)
 
-    def layer(item):
-        return 1 - zl if item % 2 == 0 else zl
-
-    def products(item):
-        child = item // 2
-
+    z_items = (3,)
+
+    def products(child, layer):
         def one(j, carry):
-            q = ((x + 6 - j) % 4) * 2 + layer(item)
+            q = ((x + 6 - j) % 4) * 2 + (zl + 1 + layer) % 2
             result = jnp.dot(acat[child], pcat[child, q], preferred_element_type=F32)
-            w[item, j, 0] = result[:, 0:128]
-            w[item, j, 1] = result[:, 128:256]
+            for block in range(2):
+                item = 2 * child + block
+                rows = slice(block * 256, block * 256 + 256)
+                w[item, layer, j, 0] = result[rows, 0:128]
+                w[item, layer, j, 1] = result[rows, 128:256]
+                remote(
+                    w.at[item, layer, j, 1 - co], sr.at[item, layer, j], sib_send.at[item, layer, j],
+                    sib_recv.at[item, layer, j], sibling,
+                ).start()
+            return carry
+
+        lax.fori_loop(0, 4, one, 0)
+
+    def chip_sum(item, layer, j):
+        wait_bytes(sr.at[item, layer, j], sib_recv.at[item, layer, j])
+        total = sr[item, layer, j] + w[item, layer, j, co]
+        if item in z_items and layer == 1:
+            wait_bytes(zq.at[item, j], zq_recv.at[item, j])
+            total = total + zq[item, j]
+        sr[item, layer, j] = total
+
+    def z_first(item):
+        for j in (0, 1, 3, 2):
+            chip_sum(item, 0, j)
             remote(
-                w.at[item, j, 1 - co], sr.at[item, j], sib_send.at[item, j],
-                sib_recv.at[item, j], sibling,
+                sr.at[item, 0, j], zq.at[item, j], zq_send.at[item, j], zq_recv.at[item, j], zpartner
             ).start()
-            return carry
-
-        lax.fori_loop(0, 4, one, 0)
-
-    def chip_sum(item, j):
-        wait_bytes(sr.at[item, j], sib_recv.at[item, j])
-        sr[item, j] = sr[item, j] + w[item, j, co]
-
-    def x_first(item):
-        chip_sum(item, 0)
-        remote(
-            sr.at[item, 0, pl.ds(0, 256), :], x1.at[item, 0], x1_send.at[item, 0],
-            x1_recv.at[item, 0], xright,
-        ).start()
-        remote(
-            sr.at[item, 0, pl.ds(256, 256), :], x1.at[item, 1], x1_send.at[item, 1],
-            x1_recv.at[item, 1], xleft,
-        ).start()
-
-    def x_second(item):
-        chip_sum(item, 1)
-        wait_bytes(x1.at[item, 0], x1_recv.at[item, 0])
-        sr[item, 1, 0:256, :] = sr[item, 1, 0:256, :] + x1[item, 0]
-        remote(
-            sr.at[item, 1], x2.at[item, 0], x2_send.at[item, 0],
-            x2_recv.at[item, 0], xright,
-        ).start()
-        chip_sum(item, 3)
-        wait_bytes(x1.at[item, 1], x1_recv.at[item, 1])
-        sr[item, 3, 256:512, :] = sr[item, 3, 256:512, :] + x1[item, 1]
-        remote(
-            sr.at[item, 3], x2.at[item, 1], x2_send.at[item, 1],
-            x2_recv.at[item, 1], xleft,
-        ).start()
-
-    def x_last(item):
-        child = item // 2
-        chip_sum(item, 2)
-        wait_bytes(x2.at[item, 0], x2_recv.at[item, 0])
-        wait_bytes(x2.at[item, 1], x2_recv.at[item, 1])
-        total = sr[item, 2] + x2[item, 0] + x2[item, 1]
-        if item % 2 == 0:
-            zs[child] = total
+
+    def x_first(item, layer):
+        chip_sum(item, layer, 0)
+        for side, rows, to in ((0, pl.ds(0, 128), xright), (1, pl.ds(128, 128), xleft)):
             remote(
-                zs.at[child], zr.at[child], z_send.at[child], z_recv.at[child], zpartner
+                sr.at[item, layer, 0, rows, :], x1.at[item, layer, side],
+                x1_send.at[item, layer, side], x1_recv.at[item, layer, side], to,
             ).start()
+
+    def x_second(item, layer):
+        for side, j, to in ((0, 1, xright), (1, 3, xleft)):
+            chip_sum(item, layer, j)
+            rows = slice(side * 128, side * 128 + 128)
+            wait_bytes(x1.at[item, layer, side], x1_recv.at[item, layer, side])
+            sr[item, layer, j, rows, :] = sr[item, layer, j, rows, :] + x1[item, layer, side]
+            remote(
+                sr.at[item, layer, j], x2.at[item, layer, side],
+                x2_send.at[item, layer, side], x2_recv.at[item, layer, side], to,
+            ).start()
+
+    def x_last(item, layer):
+        chip_sum(item, layer, 2)
+        for side in range(2):
+            wait_bytes(x2.at[item, layer, side], x2_recv.at[item, layer, side])
+        total = sr[item, layer, 2] + x2[item, layer, 0] + x2[item, layer, 1]
+        if layer == 0:
+            zs[item] = total
+            remote(zs.at[item], zr.at[item], z_send.at[item], z_recv.at[item], zpartner).start()
         else:
-            wait_bytes(zr.at[child], z_recv.at[child])
-            c_out[child] = (total + zr[child]).reshape(2, BLOCK, 128)
-
-    def c_spread(child):
-        def one(u, carry):
-            source = c_out.at[child, :, pl.ds(u * 16, 16), :]
-            target = c1[child].at[pl.ds(c * 2, 2)]
+            if item not in z_items:
+                wait_bytes(zr.at[item], z_recv.at[item])
+                total = total + zr[item]
+            c_out[item // 2, item % 2] = total
+
+    def c_spread(item):
+        child, block = item // 2, item % 2
+
+        def one(k, carry):
+            u = (c + k) % 16
+            source = c_out.at[child, block, pl.ds(u * 16, 16), :]
+            target = c1[child].at[c * 2 + block]
 
             @pl.when((r != c) | (u != r))
             def _():
@@ -270,7 +275,7 @@
 
         @pl.when(r == c)
         def _():
-            c1[child][pl.ds(c * 2, 2)] = c_out[child, :, pl.ds(r * 16, 16), :]
+            c1[child][c * 2 + block] = c_out[child, block, pl.ds(r * 16, 16), :]
 
     def c_wait(child, sem):
         @pl.when(r == c)
@@ -292,32 +297,35 @@
         ccat[child, :, 256:512] = high
         ccat[child, :, 512:768] = low
 
-        def one(q, carry):
+        def one(k, carry):
+            q = term_place(k)
             result = jnp.dot(ccat[child], pcat[child, q], preferred_element_type=F32)
-            tw[child, 0, q] = result[:, 0:128]
-            tw[child, 1, q] = result[:, 128:256]
-            return carry
-
-        lax.fori_loop(0, 8, one, 0)
-        remote(
-            tw.at[child, 1 - co], tr.at[child], tr_send.at[child], tr_recv.at[child], sibling
-        ).start()
-
-    def terms_spread(child):
-        wait_bytes(tr.at[child], tr_recv.at[child])
-        ts[child] = tw[child, co] + tr[child]
-        mine = r // 2
-
-        def one(k, carry):
-            to = (mine + k) % 8
+            tw[child, q, 0] = result[:, 0:128]
+            tw[child, q, 1] = result[:, 128:256]
             remote(
-                ts.at[child, to], tf.at[child, mine], tf_send.at[child],
-                tf_recv.at[child], (to * 2 + co, c),
+                tw.at[child, q, 1 - co], tr.at[child, q], tr_send.at[child, k],
+                tr_recv.at[child, k], sibling,
             ).start()
             return carry
 
-        lax.fori_loop(1, 8, one, 0)
-        tf[child, mine] = ts[child, mine]
+        lax.fori_loop(0, 8, one, 0)
+
+    def term_place(k):
+        return ((x + 2 + k) % 4) * 2 + (zl + 1 + k // 4) % 2
+
+    def terms_spread(child):
+        for k in (0, 1, 3, 2, 4, 5, 7, 6):
+            q = term_place(k)
+            wait_bytes(tr.at[child, q], tr_recv.at[child, k])
+            total = tw[child, q, co] + tr[child, q]
+            if k == 6:
+                tf[child, r // 2] = total
+            else:
+                ts[child, q] = total
+                remote(
+                    ts.at[child, q], tf.at[child, r // 2], tf_send.at[child],
+                    tf_recv.at[child], (q * 2 + co, c),
+                ).start()
 
     def diagonal(child):
         wait_bytes(tf.at[child, pl.ds(0, 7)], tf_recv.at[child])
@@ -335,19 +343,26 @@
         wait_bytes(pg.at[pl.ds(0, 12), child], py_send.at[child])
 
     def r_sent(child):
-        wait_bytes(zs.at[child], z_send.at[child])
         for item in (2 * child, 2 * child + 1):
-            for j in range(4):
-                wait_bytes(sr.at[item, j], sib_send.at[item, j])
-            for side in range(2):
-                wait_bytes(x1.at[item, side], x1_send.at[item, side])
-                wait_bytes(x2.at[item, side], x2_send.at[item, side])
+            for layer in range(2):
+                for j in range(4):
+                    wait_bytes(sr.at[item, layer, j], sib_send.at[item, layer, j])
+            if item in z_items:
+                for j in range(4):
+                    wait_bytes(zq.at[item, j], zq_send.at[item, j])
+            else:
+                wait_bytes(zs.at[item], z_send.at[item])
+            for layer in (1,) if item in z_items else (0, 1):
+                for side in range(2):
+                    wait_bytes(x1.at[item, layer, side], x1_send.at[item, layer, side])
+                    wait_bytes(x2.at[item, layer, side], x2_send.at[item, layer, side])
 
     def c_sent(child):
         c_wait(child, c1_send.at[child])
 
     def t_sent(child):
-        wait_bytes(tr.at[child], tr_send.at[child])
+        for k in range(8):
+            wait_bytes(tr.at[child, k], tr_send.at[child, k])
         wait_bytes(tf.at[child, pl.ds(0, 7)], tf_send.at[child])
 
     own()
@@ -374,37 +389,49 @@
     a_list(0)
     a_list(1)
     p_ready(0)
-    products(0)
-    x_first(0)
+    products(0, 0)
+    x_first(0, 0)
+    x_first(1, 0)
     p_z_pass(1)
     p_y(1, 1)
     p_y(1, 2)
-    products(1)
-    x_first(1)
+    products(0, 1)
+    x_first(0, 1)
+    x_first(1, 1)
     p_z_last(1)
     p_y(1, 3)
     p_y_pass(1, 0)
-    x_second(0)
+    x_second(0, 0)
+    x_second(1, 0)
     p_y_pass(1, 1)
     p_y_pass(1, 2)
-    x_second(1)
-    x_last(0)
+    x_second(0, 1)
+    x_second(1, 1)
+    x_last(0, 0)
+    x_last(1, 0)
     p_y_pass(1, 3)
-    x_last(1)
+    x_last(0, 1)
     c_spread(0)
+    x_last(1, 1)
+    c_spread(1)
     p_ready(1)
-    products(2)
-    x_first(2)
-    products(3)
-    x_first(3)
-    x_second(2)
+    products(1, 0)
+    x_first(2, 0)
+    z_first(3)
+    products(1, 1)
+    x_first(2, 1)
+    x_first(3, 1)
+    x_second(2, 0)
+    x_second(2, 1)
+    x_second(3, 1)
+    x_last(2, 0)
+    x_last(2, 1)
+    c_spread(2)
+    x_last(3, 1)
+    c_spread(3)
     c_ready(0)
-    x_second(3)
     terms(0)
-    x_last(2)
     terms_spread(0)
-    x_last(3)
-    c_spread(1)
     diagonal(0)
     c_ready(1)
     terms(1)
@@ -437,17 +464,18 @@
             pltpu.VMEM((2, 512, 768), BF16),
             pltpu.VMEM((16, 2, 256, 128), F32),
             pltpu.VMEM((2, 8, 768, 256), BF16),
-            pltpu.VMEM((4, 4, 2, 512, 128), F32),
-            pltpu.VMEM((4, 4, 512, 128), F32),
-            pltpu.VMEM((4, 2, 256, 128), F32),
-            pltpu.VMEM((4, 2, 512, 128), F32),
-            pltpu.VMEM((2, 512, 128), F32),
-            pltpu.VMEM((2, 512, 128), F32),
+            pltpu.VMEM((4, 2, 4, 2, 256, 128), F32),
+            pltpu.VMEM((4, 2, 4, 256, 128), F32),
+            pltpu.VMEM((4, 2, 2, 128, 128), F32),
+            pltpu.VMEM((4, 2, 2, 256, 128), F32),
+            pltpu.VMEM((4, 256, 128), F32),
+            pltpu.VMEM((4, 256, 128), F32),
+            pltpu.VMEM((4, 4, 256, 128), F32),
             pltpu.VMEM((32, 16, 128), F32),
             pltpu.VMEM((32, 16, 128), F32),
             pltpu.VMEM((2, 256, 128), F32),
             pltpu.VMEM((2, 128, 768), BF16),
-            pltpu.VMEM((2, 2, 8, 128, 128), F32),
+            pltpu.VMEM((2, 8, 2, 128, 128), F32),
             pltpu.VMEM((2, 8, 128, 128), F32),
             pltpu.VMEM((2, 8, 128, 128), F32),
             pltpu.VMEM((2, 8, 128, 128), F32),
@@ -456,12 +484,13 @@
             dma((2,)), dma((2,)),
             dma((2,)), dma((2, 2)), dma((2, 2)),
             dma((2,)), dma((2, 4, 2)), dma((2, 4, 2)),
+            dma((4, 2, 4)), dma((4, 2, 4)),
+            dma((4, 2, 2)), dma((4, 2, 2)),
+            dma((4, 2, 2)), dma((4, 2, 2)),
+            dma((4,)), dma((4,)),
             dma((4, 4)), dma((4, 4)),
-            dma((4, 2)), dma((4, 2)),
-            dma((4, 2)), dma((4, 2)),
             dma((2,)), dma((2,)),
-            dma((2,)), dma((2,)),
-            dma((2,)), dma((2,)),
+            dma((2, 8)), dma((2, 8)),
             dma((2,)), dma((2,)),
         ],
         compiler_params=pltpu.CompilerParams(

time: 125 us -> 118 us (0.944)
  Pallas kernels: 120 us -> 113 us
    pallas_call x1, Pallas kernels: 120 us -> 113 us  [body(): pl.pallas_call(kernel, out_shape=(jax.ShapeDtypeStruct((2, 2, BLOCK, 128)...]
where the time goes in v3:
time: 118 us
  Pallas kernels  113 us (96%)
  local copies, waits for them, and re-layouts  3.98 us (3%)
    pallas_call x1, Pallas kernels, body(): pl.pallas_call(kernel, out_shape=(jax.ShapeDtypeStruct((2, 2, BLOCK, 128)...  113 us
    unnamed x8, local copies, waits for them, and re-layouts  3.98 us

profile of v3, /device:TPU:1, one launch (start us, length us, event | category | flops | bytes accessed | tf_op | source)
XLA Modules:
  0.0 118.0 jit_solution(15356852867402409653)
XLA Ops:
  0.6 0.0 copy-start.2
  0.6 0.7 copy-done.2
  1.3 0.0 copy-start
  1.3 0.9 copy-done
  2.3 0.0 copy-start.1
  2.3 0.9 copy-done.1
  3.2 113.4 %shard_map.59 = (f32[2,2,256,128]{3,2,1,0:T(8,128)S(1)}, f32[2,128,128]{2,1,0:T(8,128)S(1)}) custom-call(s32[2,16]{1,0:T(2,128)S(1)} %copy-done.2, f32[2,256,512]{2,1,0:T(8,128)} %bitcast.3, f32[2,256,128]{2,1,0:T(8,128)S(1)} %copy-done, f32[2,128,128]{2,1,0:T(8,128)S(1)} %copy-done.1), custom_call_target="tpu_custom_call" | custom-call | flops 4026531840 | bytes 4194304 | tf_op jit(solution)/shard_map/pallas_call | solution.py:453
  116.6 0.8 copy.8
  117.4 0.7 copy.9
Async XLA Ops:
  0.6 0.7 copy-start.2
  1.3 0.9 copy-start
  2.3 0.9 copy-start.1

commit v4 on v3

--- a/solution.py
+++ b/solution.py
@@ -18,7 +18,7 @@
 
 
 def kernel(
-    rows_ref, a_ref, p_ref, b_ref, c_out, d_out,
+    rows_ref, a_ref, p_ref, b_ref, c_out, d_out, binv,
     a1, a2, acat, pg, pcat, w, sr, x1, x2, zs, zr, zq,
     c1a, c1b, c2, ccat, tw, tr, ts, tf,
     own_sem, a1_send, a1_recv, pa_send, pa_recv, pz_send, pz_recv, pzh_recv,
@@ -63,22 +63,7 @@
     for plane in (zup, zdown, yup, ydown):
         pl.semaphore_signal(barrier, inc=1, device_id=(r, plane), device_id_type=MESH)
 
-    def greet_senders(k, carry):
-        @pl.when((r != c) | (k != c))
-        def _():
-            pl.semaphore_signal(barrier, inc=1, device_id=(c, k), device_id_type=MESH)
-
-        return carry
-
-    lax.fori_loop(0, 16, greet_senders, 0)
-
-    @pl.when(r == c)
-    def _():
-        pl.semaphore_wait(barrier, 34)
-
-    @pl.when(r != c)
-    def _():
-        pl.semaphore_wait(barrier, 35)
+    pl.semaphore_wait(barrier, 19)
 
     def a_spread():
         lax.fori_loop(1, 16, a_spread_one, 0)
@@ -156,12 +141,14 @@
         for child in range(2)
     ]
 
+    b_own = pltpu.make_async_copy(b_ref, binv, own_sem.at[3])
+
     def own():
-        for copy in (p_mine[0], p_mine[1], a_own):
+        for copy in (p_mine[0], p_mine[1], a_own, b_own):
             copy.start()
 
     def own_ready():
-        for copy in (p_mine[0], p_mine[1], a_own):
+        for copy in (p_mine[0], p_mine[1], a_own, b_own):
             copy.wait()
 
     def a_gathered():
@@ -194,20 +181,35 @@
 
     def products(child, layer):
         def one(j, carry):
-            q = ((x + 6 - j) % 4) * 2 + (zl + 1 + layer) % 2
-            result = jnp.dot(acat[child], pcat[child, q], preferred_element_type=F32)
-            for block in range(2):
-                item = 2 * child + block
-                rows = slice(block * 256, block * 256 + 256)
-                w[item, layer, j, 0] = result[rows, 0:128]
-                w[item, layer, j, 1] = result[rows, 128:256]
-                remote(
-                    w.at[item, layer, j, 1 - co], sr.at[item, layer, j], sib_send.at[item, layer, j],
-                    sib_recv.at[item, layer, j], sibling,
-                ).start()
+            product(child, layer, j)
             return carry
 
         lax.fori_loop(0, 4, one, 0)
+
+    def product(child, layer, j):
+        q = ((x + 6 - j) % 4) * 2 + (zl + 1 + layer) % 2
+        result = jnp.dot(acat[child], pcat[child, q], preferred_element_type=F32)
+        for block in range(2):
+            item = 2 * child + block
+            rows = slice(block * 256, block * 256 + 256)
+            w[item, layer, j, 0] = result[rows, 0:128]
+            w[item, layer, j, 1] = result[rows, 128:256]
+            remote(
+                w.at[item, layer, j, 1 - co], sr.at[item, layer, j], sib_send.at[item, layer, j],
+                sib_recv.at[item, layer, j], sibling,
+            ).start()
+
+    def products_first(child):
+        block_x, block_z = 2 * child, 2 * child + 1
+        last = None
+        for j in (0, 1, 3, 2):
+            product(child, 0, j)
+            if last is not None:
+                z_send_on(block_z, last)
+            if j == 3:
+                x_first(block_x, 0)
+            last = j
+        z_send_on(block_z, last)
 
     def chip_sum(item, layer, j):
         wait_bytes(sr.at[item, layer, j], sib_recv.at[item, layer, j])
@@ -217,12 +219,11 @@
             total = total + zq[item, j]
         sr[item, layer, j] = total
 
-    def z_first(item):
-        for j in (0, 1, 3, 2):
-            chip_sum(item, 0, j)
-            remote(
-                sr.at[item, 0, j], zq.at[item, j], zq_send.at[item, j], zq_recv.at[item, j], zpartner
-            ).start()
+    def z_send_on(item, j):
+        chip_sum(item, 0, j)
+        remote(
+            sr.at[item, 0, j], zq.at[item, j], zq_send.at[item, j], zq_recv.at[item, j], zpartner
+        ).start()
 
     def x_first(item, layer):
         chip_sum(item, layer, 0)
@@ -332,7 +333,7 @@
         total = tf[child, 0]
         for k in range(1, 8):
             total = total + tf[child, k]
-        d_out[child] = b_ref[child] - total
+        d_out[child] = binv[child] - total
 
     def a_sent():
         wait_bytes(a1.at[pl.ds(0, 30)], a1_send)
@@ -388,13 +389,13 @@
     a_gathered()
     a_list(0)
     a_list(1)
+    p_z_pass(1)
+    p_y(1, 1)
+    p_y(1, 2)
     p_ready(0)
     products(0, 0)
     x_first(0, 0)
     x_first(1, 0)
-    p_z_pass(1)
-    p_y(1, 1)
-    p_y(1, 2)
     products(0, 1)
     x_first(0, 1)
     x_first(1, 1)
@@ -415,9 +416,7 @@
     x_last(1, 1)
     c_spread(1)
     p_ready(1)
-    products(1, 0)
-    x_first(2, 0)
-    z_first(3)
+    products_first(1)
     products(1, 1)
     x_first(2, 1)
     x_first(3, 1)
@@ -456,9 +455,10 @@
             jax.ShapeDtypeStruct((2, 2, BLOCK, 128), F32),
             jax.ShapeDtypeStruct((2, 128, 128), F32),
         ),
-        in_specs=[pl.BlockSpec(memory_space=pltpu.SMEM), hbm, hbm, vmem],
+        in_specs=[pl.BlockSpec(memory_space=pltpu.SMEM), hbm, hbm, hbm],
         out_specs=(vmem, vmem),
         scratch_shapes=[
+            pltpu.VMEM((2, 128, 128), F32),
             pltpu.VMEM((32, 16, 512), F32),
             pltpu.VMEM((2, 256, 512), F32),
             pltpu.VMEM((2, 512, 768), BF16),
@@ -479,7 +479,7 @@
             pltpu.VMEM((2, 8, 128, 128), F32),
             pltpu.VMEM((2, 8, 128, 128), F32),
             pltpu.VMEM((2, 8, 128, 128), F32),
-            dma((3,)),
+            dma((4,)),
             dma, dma,
             dma((2,)), dma((2,)),
             dma((2,)), dma((2, 2)), dma((2, 2)),
@@ -494,7 +494,7 @@
             dma((2,)), dma((2,)),
         ],
         compiler_params=pltpu.CompilerParams(
-            collective_id=0, has_side_effects=True, vmem_limit_bytes=52 * 1024 * 1024
+            collective_id=0, has_side_effects=True, vmem_limit_bytes=63 * 1024 * 1024
         ),
         cost_estimate=pl.CostEstimate(
             flops=3 * 2 * 2 * 256 * 2048 * (512 + 128), bytes_accessed=4 << 20, transcendentals=0

time: 118 us -> 118 us (level)
  Pallas kernels: 113 us -> 115 us
  local copies, waits for them, and re-layouts: 3.98 us -> 2.56 us
    unnamed x8 -> x4, local copies, waits for them, and re-layouts: 3.98 us -> 2.56 us
where the time goes in v4:
time: 118 us
  Pallas kernels  115 us (97%)
  local copies, waits for them, and re-layouts  2.56 us (2%)
    pallas_call x1, Pallas kernels, body(): pl.pallas_call(kernel, out_shape=(jax.ShapeDtypeStruct((2, 2, BLOCK, 128)...  115 us
    unnamed x4, local copies, waits for them, and re-layouts  2.56 us

profile of v4, /device:TPU:1, one launch (start us, length us, event | category | flops | bytes accessed | tf_op | source)
XLA Modules:
  0.0 117.7 jit_solution(8421972018344756671)
XLA Ops:
  0.6 114.5 %shard_map.59 = (f32[2,2,256,128]{3,2,1,0:T(8,128)}, f32[2,128,128]{2,1,0:T(8,128)}) custom-call(s32[2,16]{1,0:T(2,128)} %rows_ref.1, f32[2,256,512]{2,1,0:T(8,128)} %bitcast.3, f32[2,256,128]{2,1,0:T(8,128)} %p_ref.1, f32[2,128,128]{2,1,0:T(8,128)} %b_ref.1), custom_call_target="tpu_custom_call" | custom-call | flops 4026531840 | bytes 4194304 | tf_op jit(solution)/shard_map/pallas_call | solution.py:452
  115.1 0.0 copy-start
  115.2 1.9 %copy.8 = f32[2,512,128]{2,1,0:T(8,128)} copy(f32[2,512,128]{2,1,0:T(8,128)} %bitcast.2) | data formatting | bytes 1048576
  117.1 0.0 copy-done
  117.1 0.7 copy.9
Async XLA Ops:
  115.1 1.9 %copy-start = (f32[2,128,128]{2,1,0:T(8,128)S(1)}, f32[2,128,128]{2,1,0:T(8,128)}, u32[]{:S(2)}) copy-start(f32[2,128,128]{2,1,0:T(8,128)} %get-tuple-element.9) | copy-start | bytes 393220

commit v5 on v4

--- a/solution.py
+++ b/solution.py
@@ -177,7 +177,7 @@
 
         lax.fori_loop(0, 8, pair, 0)
 
-    z_items = (3,)
+    z_items = (1, 3)
 
     def products(child, layer):
         def one(j, carry):
@@ -395,7 +395,8 @@
     p_ready(0)
     products(0, 0)
     x_first(0, 0)
-    x_first(1, 0)
+    for j in (0, 1, 3, 2):
+        z_send_on(1, j)
     products(0, 1)
     x_first(0, 1)
     x_first(1, 1)
@@ -403,13 +404,11 @@
     p_y(1, 3)
     p_y_pass(1, 0)
     x_second(0, 0)
-    x_second(1, 0)
     p_y_pass(1, 1)
     p_y_pass(1, 2)
     x_second(0, 1)
     x_second(1, 1)
     x_last(0, 0)
-    x_last(1, 0)
     p_y_pass(1, 3)
     x_last(0, 1)
     c_spread(0)

time: 118 us -> 116 us (0.983)
  Pallas kernels: 115 us -> 113 us
    pallas_call x1, Pallas kernels: 115 us -> 113 us  [body(): pl.pallas_call(kernel, out_shape=(jax.ShapeDtypeStruct((2, 2, BLOCK, 128)...]
where the time goes in v5:
time: 116 us
  Pallas kernels  113 us (97%)
  local copies, waits for them, and re-layouts  2.56 us (2%)
    pallas_call x1, Pallas kernels, body(): pl.pallas_call(kernel, out_shape=(jax.ShapeDtypeStruct((2, 2, BLOCK, 128)...  113 us
    unnamed x4, local copies, waits for them, and re-layouts  2.56 us

profile of v5, /device:TPU:1, one launch (start us, length us, event | category | flops | bytes accessed | tf_op | source)
XLA Modules:
  0.0 115.8 jit_solution(13300270328298840571)
XLA Ops:
  0.6 112.6 %shard_map.59 = (f32[2,2,256,128]{3,2,1,0:T(8,128)}, f32[2,128,128]{2,1,0:T(8,128)}) custom-call(s32[2,16]{1,0:T(2,128)} %rows_ref.1, f32[2,256,512]{2,1,0:T(8,128)} %bitcast.3, f32[2,256,128]{2,1,0:T(8,128)} %p_ref.1, f32[2,128,128]{2,1,0:T(8,128)} %b_ref.1), custom_call_target="tpu_custom_call" | custom-call | flops 4026531840 | bytes 4194304 | tf_op jit(solution)/shard_map/pallas_call | solution.py:451
  113.2 0.0 copy-start
  113.2 1.9 %copy.8 = f32[2,512,128]{2,1,0:T(8,128)} copy(f32[2,512,128]{2,1,0:T(8,128)} %bitcast.2) | data formatting | bytes 1048576
  115.1 0.0 copy-done
  115.1 0.7 copy.9
Async XLA Ops:
  113.2 1.9 %copy-start = (f32[2,128,128]{2,1,0:T(8,128)S(1)}, f32[2,128,128]{2,1,0:T(8,128)}, u32[]{:S(2)}) copy-start(f32[2,128,128]{2,1,0:T(8,128)} %get-tuple-element.9) | copy-start | bytes 393220

commit v6 on v5

--- a/solution.py
+++ b/solution.py
@@ -408,8 +408,8 @@
     p_y_pass(1, 2)
     x_second(0, 1)
     x_second(1, 1)
+    p_y_pass(1, 3)
     x_last(0, 0)
-    p_y_pass(1, 3)
     x_last(0, 1)
     c_spread(0)
     x_last(1, 1)

time: 116 us -> 116 us (level)
  no operation moved by 1% of the time
where the time goes in v6:
time: 116 us
  Pallas kernels  113 us (97%)
  local copies, waits for them, and re-layouts  2.56 us (2%)
    pallas_call x1, Pallas kernels, body(): pl.pallas_call(kernel, out_shape=(jax.ShapeDtypeStruct((2, 2, BLOCK, 128)...  113 us
    unnamed x4, local copies, waits for them, and re-layouts  2.56 us

profile of v6, /device:TPU:1, one launch (start us, length us, event | category | flops | bytes accessed | tf_op | source)
XLA Modules:
  0.0 116.1 jit_solution(13903650096124655544)
XLA Ops:
  0.6 112.8 %shard_map.59 = (f32[2,2,256,128]{3,2,1,0:T(8,128)}, f32[2,128,128]{2,1,0:T(8,128)}) custom-call(s32[2,16]{1,0:T(2,128)} %rows_ref.1, f32[2,256,512]{2,1,0:T(8,128)} %bitcast.3, f32[2,256,128]{2,1,0:T(8,128)} %p_ref.1, f32[2,128,128]{2,1,0:T(8,128)} %b_ref.1), custom_call_target="tpu_custom_call" | custom-call | flops 4026531840 | bytes 4194304 | tf_op jit(solution)/shard_map/pallas_call | solution.py:451
  113.5 0.0 copy-start
  113.5 1.9 %copy.8 = f32[2,512,128]{2,1,0:T(8,128)} copy(f32[2,512,128]{2,1,0:T(8,128)} %bitcast.2) | data formatting | bytes 1048576
  115.4 0.0 copy-done
  115.4 0.7 copy.9
Async XLA Ops:
  113.5 1.9 %copy-start = (f32[2,128,128]{2,1,0:T(8,128)S(1)}, f32[2,128,128]{2,1,0:T(8,128)}, u32[]{:S(2)}) copy-start(f32[2,128,128]{2,1,0:T(8,128)} %get-tuple-element.9) | copy-start | bytes 393220
